TPU v7x, 128 devices: a whole 4x4x4 slice. The times are simulated.
128 devices in a mesh: group: 16 (over x, z), local: 8 (over y, core).
Axes of the slice: x: 4, y: 4, z: 4, core: 2. Of those that a mesh axis runs over, the one named last changes fastest.
Arguments:
- tokens: bfloat16 [16384, 4096], P(('group', 'local')), may hold values from -6 to 6
- expert_ids: int32 [16384, 2], P(('group', 'local')), may hold values from 0 to 63, all different within a row; in each aligned block of 128 rows (0 to 127, 128 to 255, ...) at most 6 rows name the same one
- gate_scores: float32 [16384, 2], P(('group', 'local')), may hold values from 0.1 to 1
- w_gate: bfloat16 [128, 4096, 768], P(('group', 'local')), may hold values from -0.09375 to 0.09375
- w_up: bfloat16 [128, 4096, 768], P(('group', 'local')), may hold values from -0.09375 to 0.09375
- w_down: bfloat16 [128, 768, 4096], P(('group', 'local')), may hold values from -0.15625 to 0.15625
Outputs:
- mixed: bfloat16 [16384, 4096], P(('group', 'local'))
Inputs may be any that keep to these rules, and one draw needn't show every extreme that they name: `expert_ids`: among the 128 rows of one device (aligned blocks), each row names 2 different experts, and no expert is named by more than 6 rows of the block; some expert reaches 6 rows.
All inputs are finite; a program needn't handle non-finite values.
Results may differ from a plain program's by a relative error of at most 0.0065.
Values may be sent and summed in bfloat16 or wider, within the bound.
A program may use at most 128 MiB of HBM per device.

v0:
```python
import jax
import jax.numpy as jnp
from jax import lax
from jax.experimental import pallas as pl
from jax.experimental.pallas import tpu as pltpu
from jax.sharding import PartitionSpec as P

MESH = pl.DeviceIdType.MESH
BF16, F32 = jnp.bfloat16, jnp.float32

SIDE = 4
CHIPS = SIDE**3
CAP = 6
GROUPS = 4
SLOTS = CHIPS // GROUPS
CHUNK = 512
PIECES = 8
PAIRS = CAP // 2
LANES = PAIRS * CHUNK
SIDES = 4
HALF = PIECES // SIDES * CHUNK
OWN = SLOTS * CAP
STRIDE = 13
EARLY = 1


def shift_of(slot):
    return 1 + lax.rem((slot + EARLY) * STRIDE, CHIPS - 1)


def kernel(
    ids_hbm, scores_hbm, tok_hbm, gate_hbm, up_hbm, down_hbm, out,
    ids, scores, tok, w_gate, w_up, w_down,
    sent, got, rows, hidden, part_own, part_out, part_in, answer, back,
    pick, mixing, spread, unspread, stage, flat, total,
    load_sem, there_send, there_recv, row_send, row_recv, part_send, part_recv, back_send, back_recv, own_sem,
):
    group, local = lax.axis_index("group"), lax.axis_index("local")
    x, z = lax.div(group, SIDE), lax.rem(group, SIDE)
    y, core = lax.div(local, 2), lax.rem(local, 2)
    twin = (group, local + 1 - 2 * core)

    def partner(slot, sign):
        shift = shift_of(slot)
        far_x = lax.rem(x + SIDE + sign * lax.div(shift, SIDE * SIDE), SIDE)
        far_y = lax.rem(y + SIDE + sign * lax.rem(lax.div(shift, SIDE), SIDE), SIDE)
        far_z = lax.rem(z + SIDE + sign * lax.rem(shift, SIDE), SIDE)
        return (far_x * SIDE + far_z, far_y * 2 + core)

    def loads():
        pairs = (
            (ids_hbm, ids), (scores_hbm, scores), (tok_hbm, tok),
            (gate_hbm.at[0], w_gate), (up_hbm.at[0], w_up), (down_hbm.at[0], w_down),
        )
        return [pltpu.make_async_copy(a, b, load_sem.at[n]) for n, (a, b) in enumerate(pairs)]

    barrier = pltpu.get_barrier_semaphore()

    for copy in loads()[:3]:
        copy.start()
    along = [[lax.rem(v + d, SIDE) for d in range(SIDE)] for v in (x, y, z)]
    for dx in (2, 1, 3, 0):
        for dz in (2, 1, 3, 0):
            wide = along[0][dx] * SIDE + along[2][dz]
            for dy in (2, 1, 3, 0):
                if dx or dy or dz:
                    pl.semaphore_signal(barrier, inc=1, device_id=(wide, along[1][dy] * 2 + core), device_id_type=MESH)
    pl.semaphore_signal(barrier, inc=1, device_id=twin, device_id_type=MESH)
    for copy in loads()[:2]:
        copy.wait()

    n = 2 * CHIPS
    row = lax.broadcasted_iota(jnp.int32, (n, n), 0)
    column = lax.broadcasted_iota(jnp.int32, (n, n), 1)
    slot, odd = lax.shift_right_logical(row, 1), row & 1
    shift = jnp.where(slot == CHIPS - 1, 0, shift_of(slot))
    expert = ((x + lax.shift_right_logical(shift, 4)) & 3) * 16 + ((z + shift) & 3) * 4 + ((y + lax.shift_right_logical(shift, 2)) & 3)
    first, second = expert == ids[0:1, :], expert == ids[1:2, :]
    chosen = jnp.where(first | second, 1.0, 0.0)
    earlier = jnp.where(row < column, 1.0, 0.0).astype(BF16)
    rank = jnp.dot(chosen.astype(BF16), earlier, preferred_element_type=F32)
    scale = scores[0:1, :] + scores[1:2, :]
    weight = jnp.where(first, scores[0:1, :] / scale, 0.0) + jnp.where(second, scores[1:2, :] / scale, 0.0)
    for j in range(PAIRS):
        here = jnp.where(rank == (2 * j + odd).astype(F32), chosen, 0.0)
        high = (here * weight).astype(BF16)
        low = (here * weight - high.astype(F32)).astype(BF16)
        for q in range(GROUPS):
            part = slice(2 * SLOTS * q, 2 * SLOTS * (q + 1))
            place = slice(2 * SLOTS * j, 2 * SLOTS * (j + 1))
            pick[q, place, :] = here[part].astype(BF16)
            mixing[0, q, place, :] = high[part]
            mixing[1, q, place, :] = low[part]

    m = 2 * SLOTS * PIECES
    a = lax.broadcasted_iota(jnp.int32, (m, m), 0)
    b = lax.broadcasted_iota(jnp.int32, (m, m), 1)

    def meets(a, b):
        same = (lax.shift_right_logical(a, 4) == (lax.shift_right_logical(b, 1) & 15)) & ((lax.shift_right_logical(a, 1) & 7) == lax.shift_right_logical(b, 5)) & ((a & 1) == (b & 1))
        return jnp.where(same, 1.0, 0.0).astype(BF16)

    spread[...] = meets(a, b)
    unspread[...] = meets(b, a)

    def pack(target, q):
        for j in range(PAIRS):
            lane = slice(j * CHUNK, (j + 1) * CHUNK)
            block = jnp.dot(spread[...], stage[:, lane], preferred_element_type=F32).astype(BF16)
            target[pl.ds(q * SLOTS, SLOTS), :, lane] = block.reshape(SLOTS, 2 * PIECES, CHUNK)

    def unpack(source, q, put):
        for j in range(PAIRS):
            lane = slice(j * CHUNK, (j + 1) * CHUNK)
            block = source[pl.ds(q * SLOTS, SLOTS), :, lane].reshape(m, CHUNK)
            block = jnp.dot(unspread[...], block, preferred_element_type=F32).astype(BF16)
            for c in range(PIECES):
                put(slice(2 * SLOTS * j, 2 * SLOTS * (j + 1)), slice(c * CHUNK, (c + 1) * CHUNK), block[2 * SLOTS * c : 2 * SLOTS * (c + 1)])

    def to_stage(c, value):
        for j in range(PAIRS):
            stage[2 * SLOTS * c : 2 * SLOTS * (c + 1), j * CHUNK : (j + 1) * CHUNK] = value[2 * SLOTS * j : 2 * SLOTS * (j + 1)]

    def remote(source, target, slot, sign, send, recv):
        return pltpu.make_async_remote_copy(
            src_ref=source.at[slot], dst_ref=target.at[slot], send_sem=send, recv_sem=recv,
            device_id=partner(slot, sign), device_id_type=MESH,
        )

    def send_some(source, target, q, start, stop, sign, send, recv):
        def one(i, carry):
            remote(source, target, q * SLOTS + i, sign, send, recv.at[q]).start()
            return carry

        lax.fori_loop(start, stop, one, 0)

    def keep_own(source, target):
        pltpu.make_async_copy(source.at[CHIPS - 1], target.at[CHIPS - 1], own_sem).start()

    def send_group(source, target, q, sign, send, recv):
        send_some(source, target, q, 0, SLOTS - lax.div(q, GROUPS - 1), sign, send, recv)

        @pl.when(q == GROUPS - 1)
        def _():
            keep_own(source, target)

    def wait_group(target, q, recv):
        @pl.when(q < GROUPS - 1)
        def _():
            ref = target.at[pl.ds(0, SLOTS)]
            pltpu.make_async_copy(ref, ref, recv.at[q]).wait()

        @pl.when(q == GROUPS - 1)
        def _():
            ref = target.at[pl.ds(0, SLOTS - 1)]
            pltpu.make_async_copy(ref, ref, recv.at[q]).wait()
            pltpu.make_async_copy(target.at[CHIPS - 1], target.at[CHIPS - 1], own_sem).wait()

    loads()[2].wait()

    def dispatch(t, carry):
        q = lax.rem(t + GROUPS - 1, GROUPS)
        for c in range(PIECES):
            value = jnp.dot(pick[q], tok[:, c * CHUNK : (c + 1) * CHUNK], preferred_element_type=F32)
            to_stage(c, value.astype(BF16))
        pack(sent, q)

        @pl.when(t == 0)
        def _():
            pl.semaphore_wait(barrier, CHIPS)

        start = jnp.where(t == 0, SLOTS - 1 - EARLY, 0)
        send_some(sent, got, q, start, jnp.where(t == 0, SLOTS - 1, SLOTS), 1, there_send, there_recv)
        return carry

    lax.fori_loop(0, GROUPS, dispatch, 0)
    for copy in loads()[3:]:
        copy.start()
    send_some(sent, got, GROUPS - 1, 0, SLOTS - 1 - EARLY, 1, there_send, there_recv)
    keep_own(sent, got)
    for copy in loads()[3:]:
        copy.wait()

    def to_twin(source, target, send, recv):
        return pltpu.make_async_remote_copy(
            src_ref=source, dst_ref=target, send_sem=send, recv_sem=recv, device_id=twin, device_id_type=MESH
        )

    def over_rows(q):
        return to_twin(rows.at[q, pl.ds(0, OWN)], rows.at[q, pl.ds(OWN, OWN)], row_send.at[q], row_recv.at[q])

    def over_part(q, h):
        side = pl.ds(pl.multiple_of(h * HALF, HALF), HALF)
        return to_twin(part_out.at[q, :, side], part_in.at[q, :, side], part_send.at[SIDES * q + h], part_recv.at[SIDES * q + h])

    def arrive(q):
        wait_group(got, q, there_recv)

        def put(r, c, value):
            rows[q, r, c] = value

        unpack(got, q, put)
        over_rows(q).start()

    arrive(0)

    def work(q, carry):
        over_rows(q).wait_recv()

        def up(t, carry):
            lane = pl.ds(pl.multiple_of(t * 256, 256), 256)
            gate = jnp.dot(rows[q], w_gate[:, lane], preferred_element_type=F32)
            upper = jnp.dot(rows[q], w_up[:, lane], preferred_element_type=F32)
            hidden[:, lane] = (gate / (1.0 + jnp.exp(-gate)) * upper).astype(BF16)
            return carry

        lax.fori_loop(0, 3, up, 0)

        def side(h, carry):
            def down(t, carry):
                lane = pl.ds(pl.multiple_of(h * HALF + t * CHUNK, CHUNK), CHUNK)
                part = jnp.dot(hidden[...], w_down[:, lane], preferred_element_type=F32).astype(BF16)
                part_own[:, lane] = part[:OWN]
                part_out[q, :, lane] = part[OWN:]
                return carry

            lax.fori_loop(0, PIECES // SIDES, down, 0)
            over_part(q, h).start()
            return carry

        lax.fori_loop(0, SIDES, side, 0)

        @pl.when(q < GROUPS - 1)
        def _():
            arrive(q + 1)

        for c in range(PIECES):
            if c % (PIECES // SIDES) == 0:
                over_part(q, c // (PIECES // SIDES)).wait_recv()
            lane = slice(c * CHUNK, (c + 1) * CHUNK)
            to_stage(c, (part_own[:, lane].astype(F32) + part_in[q, :, lane].astype(F32)).astype(BF16))
        pack(answer, q)
        send_group(answer, back, q, -1, back_send, back_recv)
        return carry

    lax.fori_loop(0, GROUPS, work, 0)

    total[...] = jnp.zeros_like(total)

    def finish(q, put_sum):
        wait_group(back, q, back_recv)

        def put(r, c, value):
            flat[r, c] = value

        unpack(back, q, put)
        for c in range(PIECES):
            lane = slice(c * CHUNK, (c + 1) * CHUNK)
            high, low = (
                lax.dot_general(mixing[h, q], flat[:, lane], (((0,), (0,)), ((), ())), preferred_element_type=F32)
                for h in range(2)
            )
            put_sum(lane, total[:, lane] + high + low)

    def keep(lane, value):
        total[:, lane] = value

    def leave(lane, value):
        out[:, lane] = value.astype(BF16)

    def early(q, carry):
        finish(q, keep)
        return carry

    lax.fori_loop(0, GROUPS - 1, early, 0)
    finish(GROUPS - 1, leave)
    for q in range(GROUPS):
        over_rows(q).wait_send()
        for h in range(SIDES):
            over_part(q, h).wait_send()
    for source, send in ((sent, there_send), (answer, back_send)):
        ref = source.at[pl.ds(0, CHIPS - 1)]
        pltpu.make_async_copy(ref, ref, send).wait()


def body(tokens, expert_ids, gate_scores, w_gate, w_up, w_down):
    rows, width = tokens.shape
    half = w_gate.shape[2]
    blocks = (CHIPS, 2 * PIECES, LANES)
    m = 2 * SLOTS * PIECES
    vmem, hbm = pl.BlockSpec(memory_space=pltpu.VMEM), pl.BlockSpec(memory_space=pl.ANY)
    far = pl.BlockSpec(memory_space=pltpu.HBM)
    dma = pltpu.SemaphoreType.DMA
    return pl.pallas_call(
        kernel,
        out_shape=jax.ShapeDtypeStruct((rows, width), BF16),
        in_specs=[far, far, hbm, hbm, hbm, hbm],
        out_specs=vmem,
        scratch_shapes=[
            pltpu.VMEM(expert_ids.shape[::-1], jnp.int32),
            pltpu.VMEM(gate_scores.shape[::-1], F32),
            pltpu.VMEM((rows, width), BF16),
            pltpu.VMEM((width, half), BF16),
            pltpu.VMEM((width, half), BF16),
            pltpu.VMEM((half, width), BF16),
            pltpu.VMEM(blocks, BF16),
            pltpu.VMEM(blocks, BF16),
            pltpu.VMEM((GROUPS, 2 * OWN, width), BF16),
            pltpu.VMEM((2 * OWN, half), BF16),
            pltpu.VMEM((OWN, width), BF16),
            pltpu.VMEM((GROUPS, OWN, width), BF16),
            pltpu.VMEM((GROUPS, OWN, width), BF16),
            pltpu.VMEM(blocks, BF16),
            pltpu.VMEM(blocks, BF16),
            pltpu.VMEM((GROUPS, OWN, rows), BF16),
            pltpu.VMEM((2, GROUPS, OWN, rows), BF16),
            pltpu.VMEM((m, m), BF16),
            pltpu.VMEM((m, m), BF16),
            pltpu.VMEM((m, LANES), BF16),
            pltpu.VMEM((OWN, width), BF16),
            pltpu.VMEM((rows, width), F32),
            dma((6,)),
            dma, dma((GROUPS,)),
            dma((GROUPS,)), dma((GROUPS,)),
            dma((SIDES * GROUPS,)), dma((SIDES * GROUPS,)),
            dma, dma((GROUPS,)),
            dma,
        ],
        compiler_params=pltpu.CompilerParams(collective_id=0, has_side_effects=True, vmem_limit_bytes=52 << 20),
    )(expert_ids.T, gate_scores.T, tokens, w_gate, w_up, w_down)


def solution(mesh):
    split = ("group", "local")
    flat, deep = P(split, None), P(split, None, None)
    return jax.shard_map(
        body, mesh=mesh, in_specs=(flat, flat, flat, deep, deep, deep), out_specs=flat, check_vma=False
    )
```

profile of v0, /device:TPU:1, one launch (start us, length us, event | category | flops | bytes accessed | tf_op | source)
XLA Modules:
  0.0 85.5 jit_solution(6775800365565724298)
XLA Ops:
  0.0 0.0 copy-start
  0.0 0.7 copy-done
  0.7 0.0 copy-start.1
  0.7 0.7 copy-done.1
  1.4 83.1 %shard_map.64 = bf16[128,4096]{1,0:T(8,128)(2,1)S(1)} custom-call(s32[2,128]{1,0:T(2,128)S(1)} %bitcast.2, f32[2,128]{1,0:T(2,128)S(1)} %bitcast.3, bf16[128,4096]{1,0:T(8,128)(2,1)} %tok_hbm.1, bf16[1,4096,768]{2,1,0:T(8,128)(2,1)} %gate_hbm.1, bf16[1,4096,768]{2,1,0:T(8,128)(2,1)} %up_hbm.1, bf16[1,768,4096]{2,1,0:T(8,128)(2,1)} %down_hbm.1), custom_call_target="tpu_custom_call" | custom-call | tf_op jit(solution)/shard_map/pallas_call | solution.py:294
  84.5 1.0 %copy.8 = bf16[128,4096]{1,0:T(8,128)(2,1)} copy(bf16[128,4096]{1,0:T(8,128)(2,1)S(1)} %shard_map.64) | data formatting | bytes 2097152
Async XLA Ops:
  0.0 0.7 copy-start
  0.7 0.7 copy-start.1
where the time goes:
time: 85.6 us; the launch traced here: 85.5 us
  Pallas kernels  83.1 us (97%)
  local copies, waits for them, and re-layouts  2.33 us (3%)
    pallas_call x1, Pallas kernels, body(): pl.pallas_call(kernel, out_shape=jax.ShapeDtypeStruct((rows, width), BF16...  83.1 us
    unnamed x5, local copies, waits for them, and re-layouts  2.33 us

commit v1 on v0

--- a/solution.py
+++ b/solution.py
@@ -21,11 +21,12 @@
 HALF = PIECES // SIDES * CHUNK
 OWN = SLOTS * CAP
 STRIDE = 13
+APART = 31
 EARLY = 1
 
 
-def shift_of(slot):
-    return 1 + lax.rem((slot + EARLY) * STRIDE, CHIPS - 1)
+def shift_of(slot, core):
+    return 1 + lax.rem((slot + EARLY + core * APART) * STRIDE, CHIPS - 1)
 
 
 def kernel(
@@ -41,7 +42,7 @@
     twin = (group, local + 1 - 2 * core)
 
     def partner(slot, sign):
-        shift = shift_of(slot)
+        shift = shift_of(slot, core)
         far_x = lax.rem(x + SIDE + sign * lax.div(shift, SIDE * SIDE), SIDE)
         far_y = lax.rem(y + SIDE + sign * lax.rem(lax.div(shift, SIDE), SIDE), SIDE)
         far_z = lax.rem(z + SIDE + sign * lax.rem(shift, SIDE), SIDE)
@@ -73,7 +74,7 @@
     row = lax.broadcasted_iota(jnp.int32, (n, n), 0)
     column = lax.broadcasted_iota(jnp.int32, (n, n), 1)
     slot, odd = lax.shift_right_logical(row, 1), row & 1
-    shift = jnp.where(slot == CHIPS - 1, 0, shift_of(slot))
+    shift = jnp.where(slot == CHIPS - 1, 0, shift_of(slot, core))
     expert = ((x + lax.shift_right_logical(shift, 4)) & 3) * 16 + ((z + shift) & 3) * 4 + ((y + lax.shift_right_logical(shift, 2)) & 3)
     first, second = expert == ids[0:1, :], expert == ids[1:2, :]
     chosen = jnp.where(first | second, 1.0, 0.0)

time: 85.6 us -> 86.1 us (level)
  no operation moved by 1% of the time
where the time goes in v1:
time: 86.1 us; the launch traced here: 85.9 us
  Pallas kernels  83.6 us (97%)
  local copies, waits for them, and re-layouts  2.33 us (3%)
    pallas_call x1, Pallas kernels, body(): pl.pallas_call(kernel, out_shape=jax.ShapeDtypeStruct((rows, width), BF16...  83.6 us
    unnamed x5, local copies, waits for them, and re-layouts  2.33 us

profile of v1, /device:TPU:1, one launch (start us, length us, event | category | flops | bytes accessed | tf_op | source)
XLA Modules:
  0.0 85.9 jit_solution(647804611493752125)
XLA Ops:
  0.0 0.0 copy-start
  0.0 0.7 copy-done
  0.7 0.0 copy-start.1
  0.7 0.7 copy-done.1
  1.4 83.6 %shard_map.64 = bf16[128,4096]{1,0:T(8,128)(2,1)S(1)} custom-call(s32[2,128]{1,0:T(2,128)S(1)} %bitcast.2, f32[2,128]{1,0:T(2,128)S(1)} %bitcast.3, bf16[128,4096]{1,0:T(8,128)(2,1)} %tok_hbm.1, bf16[1,4096,768]{2,1,0:T(8,128)(2,1)} %gate_hbm.1, bf16[1,4096,768]{2,1,0:T(8,128)(2,1)} %up_hbm.1, bf16[1,768,4096]{2,1,0:T(8,128)(2,1)} %down_hbm.1), custom_call_target="tpu_custom_call" | custom-call | tf_op jit(solution)/shard_map/pallas_call | solution.py:295
  84.9 1.0 %copy.8 = bf16[128,4096]{1,0:T(8,128)(2,1)} copy(bf16[128,4096]{1,0:T(8,128)(2,1)S(1)} %shard_map.64) | data formatting | bytes 2097152
Async XLA Ops:
  0.0 0.7 copy-start
  0.7 0.7 copy-start.1

commit v2 on v0

--- a/solution.py
+++ b/solution.py
@@ -56,8 +56,6 @@
 
     barrier = pltpu.get_barrier_semaphore()
 
-    for copy in loads()[:3]:
-        copy.start()
     along = [[lax.rem(v + d, SIDE) for d in range(SIDE)] for v in (x, y, z)]
     for dx in (2, 1, 3, 0):
         for dz in (2, 1, 3, 0):
@@ -66,6 +64,8 @@
                 if dx or dy or dz:
                     pl.semaphore_signal(barrier, inc=1, device_id=(wide, along[1][dy] * 2 + core), device_id_type=MESH)
     pl.semaphore_signal(barrier, inc=1, device_id=twin, device_id_type=MESH)
+    for copy in loads()[:3]:
+        copy.start()
     for copy in loads()[:2]:
         copy.wait()
 

time: 85.6 us -> 85.7 us (level)
  no operation moved by 1% of the time
where the time goes in v2:
time: 85.7 us; the launch traced here: 85.5 us
  Pallas kernels  83.1 us (97%)
  local copies, waits for them, and re-layouts  2.33 us (3%)
    pallas_call x1, Pallas kernels, body(): pl.pallas_call(kernel, out_shape=jax.ShapeDtypeStruct((rows, width), BF16...  83.1 us
    unnamed x5, local copies, waits for them, and re-layouts  2.33 us

profile of v2, /device:TPU:1, one launch (start us, length us, event | category | flops | bytes accessed | tf_op | source)
XLA Modules:
  0.0 85.5 jit_solution(12955206405931287332)
XLA Ops:
  0.0 0.0 copy-start
  0.0 0.7 copy-done
  0.7 0.0 copy-start.1
  0.7 0.7 copy-done.1
  1.4 83.1 %shard_map.64 = bf16[128,4096]{1,0:T(8,128)(2,1)S(1)} custom-call(s32[2,128]{1,0:T(2,128)S(1)} %bitcast.2, f32[2,128]{1,0:T(2,128)S(1)} %bitcast.3, bf16[128,4096]{1,0:T(8,128)(2,1)} %tok_hbm.1, bf16[1,4096,768]{2,1,0:T(8,128)(2,1)} %gate_hbm.1, bf16[1,4096,768]{2,1,0:T(8,128)(2,1)} %up_hbm.1, bf16[1,768,4096]{2,1,0:T(8,128)(2,1)} %down_hbm.1), custom_call_target="tpu_custom_call" | custom-call | tf_op jit(solution)/shard_map/pallas_call | solution.py:294
  84.5 1.0 %copy.8 = bf16[128,4096]{1,0:T(8,128)(2,1)} copy(bf16[128,4096]{1,0:T(8,128)(2,1)S(1)} %shard_map.64) | data formatting | bytes 2097152
Async XLA Ops:
  0.0 0.7 copy-start
  0.7 0.7 copy-start.1
